TPU v7x, 256 devices: a whole 4x4x8 slice. The times are simulated.
256 devices in a mesh: section: 4 (over x), dp: 16 (over z, core), tensor: 4 (over y).
Axes of the slice: x: 4, y: 4, z: 8, core: 2. Of those that a mesh axis runs over, the one named last changes fastest.
Arguments:
- acts: bfloat16 [4, 4, 16, 128, 4096], P('section', None, 'dp', None, 'tensor'), may hold values from -24 to 24
- w_qkv: bfloat16 [4, 4096, 5120], P('section', None, 'tensor'), may hold values from -2 to 2
- lengths: int32 [4, 16, 4], replicated, may hold values from 1 to 383, as said below
- block_source: int32 [4, 64], replicated, may hold values from 0 to 63, as said below
Outputs:
- context: bfloat16 [4, 8192, 4096], P('section', 'dp', 'tensor')
Inputs may be any that keep to these rules, and one draw needn't show every extreme that they name: `block_source`: for every section, each block of the sending order fills exactly one slot; the blocks of one document go to one replica; a replica takes at most 1 block held by any one index of dp, and exactly 1 from some index. The 4 lengths of each sequence sum to 512.
All inputs are finite; a program needn't handle non-finite values.
Results may differ from a plain program's by a relative error of at most 0.012.
The roundings to bfloat16 on the way count: a program that leaves them out, or rounds other values in their place, can miss the bound.
Values may be sent and summed in bfloat16 or wider, within the bound.
A program may use at most 128 MiB of HBM per device.

v0:
```python
import math

import jax
import jax.numpy as jnp
from jax import lax
from jax.sharding import PartitionSpec as P

HD = 128
HB = 128
BLK = 128
DOCS = 4
TOK_DEV = 512
GQ = 8


norm_eps = 1e-05
rope_theta = 500000.0


def shifted(value, axis, steps):
    count = lax.axis_size(axis)
    pairs = [(source, (source + steps) % count) for source in range(count)]
    return lax.ppermute(value, axis, pairs)


def hadamard(block_size):
    counter = jnp.arange(block_size, dtype=jnp.int32)
    shared_bits = jnp.bitwise_and(counter[:, None], counter[None, :])
    parity = jnp.zeros((block_size, block_size), jnp.int32)
    for bit_pos in range(block_size.bit_length()):
        parity = parity + jnp.bitwise_and(jnp.right_shift(shared_bits, bit_pos), 1)
    signs = jnp.where(parity % 2 == 0, 1.0, -1.0).astype(jnp.float32)
    return signs / math.sqrt(block_size)


def rotate_rows(values_in):
    dims_all = values_in.shape
    blocks = values_in.reshape(dims_all[:-1] + (dims_all[-1] // HB, HB))
    turned = jnp.einsum("...ij,jk->...ik", blocks, hadamard(HB), precision=lax.Precision.HIGHEST)
    return turned.reshape(dims_all)


def doc_layout(token_index, section_lengths):
    window = token_index // TOK_DEV
    offset = token_index % TOK_DEV
    doc_lengths = section_lengths[window]
    doc_ends = jnp.cumsum(doc_lengths, axis=-1)
    doc_index = jnp.sum((offset[:, None] >= doc_ends).astype(jnp.int32), axis=-1)
    starts = doc_ends - doc_lengths
    which = jnp.arange(DOCS, dtype=jnp.int32)[None, :] == doc_index[:, None]
    chosen = jnp.sum(jnp.where(which, starts, 0), axis=-1)
    return (window * DOCS + doc_index, offset - chosen)


def rotary(values_in, positions):
    half_dim = HD // 2
    steps_f = jnp.arange(half_dim, dtype=jnp.float32)
    inv_freq = jnp.exp(-math.log(rope_theta) * 2.0 * steps_f / HD)
    angles = positions.astype(jnp.float32)[:, None] * inv_freq[None, :]
    angles = angles.reshape((angles.shape[0],) + (1,) * (values_in.ndim - 2) + (half_dim,))
    cosine = jnp.cos(angles)
    sine_vals = jnp.sin(angles)
    first_half = values_in[..., :half_dim]
    second_half = values_in[..., half_dim:]
    return jnp.concatenate(
        [
            first_half * cosine - second_half * sine_vals,
            second_half * cosine + first_half * sine_vals,
        ],
        axis=-1,
    )


def reassign(own_blocks, route_plan, replicas, my_replica):
    n_blocks = own_blocks.shape[0]
    route_table = route_plan.reshape(replicas, n_blocks)
    block_owner = route_table % replicas
    block_slot = route_table // replicas
    gathered = lax.all_gather(own_blocks[None], "dp", axis=0, tiled=True)
    picked = gathered[block_owner[my_replica], block_slot[my_replica]]
    return picked


def local(acts, w_qkv, lengths, block_source):
    my_section = lax.axis_index("section")
    replicas = lax.axis_size("dp")
    my_replica = lax.axis_index("dp")
    own_blocks = rotate_rows(acts[0, :, 0].astype(jnp.float32)).astype(jnp.bfloat16)
    n_blocks = own_blocks.shape[0]
    route_plan = lax.dynamic_index_in_dim(block_source, my_section, 0, keepdims=False)
    hopped = shifted(own_blocks, "section", 1)
    arrived = reassign(hopped, route_plan, replicas, my_replica)
    received = arrived.reshape(n_blocks * BLK, arrived.shape[-1])
    row_count = received.shape[0]
    weight_cols = w_qkv[0]
    whole_rows = lax.all_gather(received, "tensor", axis=1, tiled=True)
    widened = whole_rows.astype(jnp.float32)
    square_mean = jnp.mean(widened * widened, axis=-1, keepdims=True)
    normed = (widened * lax.rsqrt(square_mean + norm_eps)).astype(jnp.bfloat16)
    projected = jnp.dot(normed, weight_cols, preferred_element_type=jnp.float32)
    groups = projected.shape[1] // ((GQ + 2) * HD)
    head_cols = projected.reshape(row_count, groups, GQ + 2, HD)
    row_blocks = lax.dynamic_slice_in_dim(route_plan, my_replica * n_blocks, n_blocks, 0)
    token_index = (row_blocks[:, None] * BLK + jnp.arange(BLK, dtype=jnp.int32)[None, :]).reshape(
        row_count
    )
    section_lengths = lax.dynamic_index_in_dim(lengths, my_section, 0, keepdims=False)
    doc_ids, positions = doc_layout(token_index, section_lengths)
    queries = rotary(head_cols[:, :, :GQ], positions).astype(jnp.bfloat16)
    key_rows = rotary(head_cols[:, :, GQ], positions).astype(jnp.bfloat16)
    value_rows = head_cols[:, :, GQ + 1].astype(jnp.bfloat16)
    score_scale = 1.0 / math.sqrt(HD)
    scores = (
        jnp.einsum("rgqd,sgd->gqrs", queries, key_rows, preferred_element_type=jnp.float32)
        * score_scale
    )
    seen = (doc_ids[:, None] == doc_ids[None, :]) & (positions[None, :] <= positions[:, None])
    row_max = jnp.max(jnp.where(seen, scores, -1e30), axis=-1, keepdims=True)
    probs = jnp.where(seen, jnp.exp(scores - row_max), 0.0)
    totals = jnp.sum(probs, axis=-1)
    probs_low = probs.astype(jnp.bfloat16)
    context = jnp.einsum(
        "gqrs,sgd->rgqd", probs_low, value_rows, preferred_element_type=jnp.float32
    )
    context = context / jnp.transpose(totals, (2, 0, 1))[..., None]
    return context.reshape(row_count, groups * GQ * HD).astype(jnp.bfloat16)[None]


def solution(mesh):
    placed = (P("section", None, "dp", None, "tensor"), P("section", None, "tensor"), P(), P())
    return jax.shard_map(
        local, mesh=mesh, in_specs=placed, out_specs=P("section", "dp", "tensor"), check_vma=False
    )
```

profile of v0, /device:TPU:8, one launch (start us, length us, event | category | flops | bytes accessed | tf_op | source)
XLA Modules:
  0.0 217.8 jit_solution(4173233659687998639)
XLA Ops:
  6.5 0.0 copy-start
  6.5 0.0 all-gather.6.cloned.1.call-start
  6.5 1.5 copy.33
  8.0 1.1 convolution_convert_fusion
  9.1 0.5 copy.21
  9.6 1.6 collective-permute-start
  11.2 24.6 %collective-permute-done = bf16[4,128,1024]{2,1,0:T(8,128)(2,1)S(1)} collective-permute-done((bf16[4,128,1024]{2,1,0:T(8,128)(2,1)S(1)}, bf16[4,128,1024]{2,1,0:T(8,128)(2,1)S(1)}, u32[]{:S(2)}, u32[]{:S(2)}) %collective-permute-start) | collective-permute-done | bytes 1048608 | tf_op jit(solution)/shard_map/ppermute | solution.py:23
  35.8 0.0 copy-start.1
  35.8 1.0 copy-done.1
  36.8 0.0 all-gather.6.cloned.1.call-update
  36.8 0.2 all-gather.4.cloned.1.call-start
  37.1 0.7 fusion.68
  37.8 0.1 reshape.471
  37.9 96.2 %all-gather.6.cloned.1.call-done = bf16[64,128,1024]{2,1,0:T(8,128)(2,1)} async-done(((bf16[4,128,1024]{2,1,0:T(8,128)(2,1)}), bf16[64,128,1024]{2,1,0:T(8,128)(2,1)}) %all-gather.6.cloned.1.call-update) | async-done | bytes 16777232 | tf_op jit(solution)/shard_map/all_gather | solution.py:79
  134.1 7.4 %gather_fusion = bf16[4,128,1024]{2,1,0:T(8,128)(2,1)} fusion(bf16[16,4,128,1024]{3,2,1,0:T(8,128)(2,1)} %bitcast.137, s32[4]{0:T(128)S(1)} %fusion.76), kind=kCustom, calls=%fused_computation | custom fusion | bytes 2097184 | tf_op jit(solution)/shard_map/gather | solution.py:80
  141.4 0.0 all-gather.4.cloned.1.call-update
  141.4 14.4 %copy.22 = bf16[1,4096,1280]{1,2,0:T(8,128)(2,1)} copy(bf16[1,4096,1280]{2,1,0:T(8,128)(2,1)} %param.5) | data formatting | bytes 20971520 | tf_op args[1]
  155.8 0.0 copy-done
  155.9 0.1 copy.23
  155.9 0.8 multiply_bitcast_fusion
  156.7 0.1 iota_add_fusion
  156.8 1.0 gather_fusion.1
  157.8 0.2 reduce_window_sum.11
  158.1 0.1 add_select_fusion.1
  158.2 0.2 convert_reduce_fusion
  158.4 0.2 select_reduce_fusion
  158.6 0.1 fusion.91
  158.7 0.5 multiply_cosine_fusion
  159.3 0.3 compare_and_fusion
  159.5 30.8 %all-gather.4.cloned.1.call-done = bf16[512,4096]{1,0:T(8,128)(2,1)} async-done(((bf16[512,1024]{1,0:T(8,128)(2,1)}), bf16[512,4096]{1,0:T(8,128)(2,1)}) %all-gather.4.cloned.1.call-update) | async-done | bytes 4194320 | tf_op jit(solution)/shard_map/all_gather | solution.py:96
  190.3 3.1 %fusion = f32[512]{0:T(512)S(1)} fusion(bf16[512,4096]{1,0:T(8,128)(2,1)} %all-gather.4.cloned.1.call-done), kind=kLoop, calls=%fused_computation.4 | loop fusion | flops 6290944 | bytes 4196352 | tf_op jit(solution)/shard_map/reduce_sum | solution.py:98
  193.4 9.8 %fusion.16 = f32[512,1,10,128]{0,3,2,1:T(8,128)S(1)} fusion(bf16[10,128,4096]{2,1,0:T(8,128)(2,1)} %bitcast.131, bf16[512,4096]{1,0:T(8,128)(2,1)} %all-gather.4.cloned.1.call-done, f32[512]{0:T(512)S(1)} %add_rsqrt_fusion), kind=kOutput, calls=%fused_computation.21 | convolution fusion | flops 5375000576 | bytes 17303552 | tf_op jit(solution)/shard_map/dot_general | solution.py:100
  203.2 0.6 fusion.46
  203.8 0.4 fusion.26
  204.2 1.6 fusion.2
  205.8 1.7 fusion.5
  207.5 2.1 fusion.15
  209.6 1.3 copy.27
  (8 shorter events, 0.1 us)
Async XLA Ops:
  6.5 149.3 %copy-start = (s32[4,16,4]{1,2,0:T(4,128)S(1)}, s32[4,16,4]{1,2,0:T(4,128)}, u32[]{:S(2)}) copy-start(s32[4,16,4]{1,2,0:T(4,128)} %param.6) | copy-start | bytes 3076
  6.5 127.5 %all-gather.6.cloned.1.call-start = ((), (), s32[]{:S(2)}) async-start(), calls=%async_computation.1 | async-start | bytes 17825792 | tf_op jit(solution)/shard_map/all_gather | solution.py:79
  9.6 26.2 %collective-permute-start = (bf16[4,128,1024]{2,1,0:T(8,128)(2,1)S(1)}, bf16[4,128,1024]{2,1,0:T(8,128)(2,1)S(1)}, u32[]{:S(2)}, u32[]{:S(2)}) collective-permute-start(bf16[4,128,1024]{2,1,0:T(8,128)(2,1)S(1)} %copy.21), channel_id=1, source_target_pairs={{0,64},{64,128},{128,192},{192,0},{1,65},{65,129},{129,193},{193,1... | collective-permute-start | bytes 3145736 | tf_op jit(solution)/shard_map/ppermute | solution.py:23
  35.8 1.0 copy-start.1
  36.8 153.5 %all-gather.4.cloned.1.call-start = ((), (), s32[]{:S(2)}) async-start(), calls=%async_computation | async-start | bytes 5242880 | tf_op jit(solution)/shard_map/all_gather | solution.py:96
Sparse Core Ops, SparseCore 0:
  36.9 97.0 all-gather.5
  141.6 48.7 all-gather.3
where the time goes:
time: 220 us; the launch traced here: 218 us
  waiting for transfers between devices  152 us (69%)
  local copies, waits for them, and re-layouts  28 us (13%)
  matrix products  14.5 us (7%)
  between operations  13.6 us (6%)
  other arithmetic  8.31 us (4%)
    all_gather x1, waiting for transfers between devices, reassign(): gathered = lax.all_gather(own_blocks[None], 'dp', axis=0, tiled=True)  96.2 us
    all_gather x1, waiting for transfers between devices, local(): whole_rows = lax.all_gather(received, 'tensor', axis=1, tiled=True)  30.8 us
    ppermute x1, waiting for transfers between devices, shifted(): return lax.ppermute(value, axis, pairs)  24.6 us
    unnamed x6, local copies, waits for them, and re-layouts  16.9 us
    dot_general x1, matrix products, local(): projected = jnp.dot(normed, weight_cols, preferred_element_type=jnp.float32)  9.76 us
    gather x1, local copies, waits for them, and re-layouts, reassign(): picked = gathered[block_owner[my_replica], block_slot[my_replica]]  7.35 us
  transfers between devices with their start and end apart: 3, of which 3 were waited for; matrix products, arithmetic and copies ran while one was open for 9% of the time, Pallas kernels for 0%

commit v1 on v0

v1 whole, which is shorter than its diff:
```python
import functools
import math

import jax
import jax.numpy as jnp
from jax import lax
from jax.experimental import pallas as pl
from jax.experimental.pallas import tpu as pltpu
from jax.sharding import PartitionSpec as P

HD = 128
HB = 128
BLK = 128
DOCS = 4
TOK_DEV = 512
GQ = 8
NB = 4
D = 4096
LOCAL = 1024
COLS = 1280
CHIPS = 8
REPL = 16
CHUNKS = 4
FEAT = LOCAL // CHUNKS
HALF = FEAT // 2
ROWS = 16
AHEAD = 2

norm_eps = 1e-05
rope_theta = 500000.0
MESH = pl.DeviceIdType.MESH


def rotated_chip(step, chip):
    distance = CHIPS // 2 - (step + 1) // 2
    sign = 2 * (step % 2) - 1
    return (chip + CHIPS + sign * distance) % CHIPS


def slot_docs(bs_ref, len_ref, section, block, offset_iota):
    window = block // NB
    base = (section * REPL + window) * DOCS
    offset = (block % NB) * BLK + offset_iota
    end = len_ref[base]
    start = jnp.zeros_like(offset)
    document = jnp.zeros_like(offset)
    for d in range(DOCS):
        past = offset >= end
        document = document + past.astype(jnp.int32)
        start = jnp.where(past, end, start)
        if d < DOCS - 1:
            end = end + len_ref[base + d + 1]
    return window * DOCS + document, offset - start


def exchange_kernel(
    sections, tensors, acts_ref, w_ref, len_ref, bs_ref, qkv_ref,
    sbuf, obuf, x, wv, acc, squares, cos_t, sin_t,
    w_sem, p1_send, p1_recv, p2_send, p2_recv, y_send, y_recv, *mid
):
    s = lax.axis_index("section")
    i = lax.axis_index("dp")
    t = lax.axis_index("tensor")
    chip, core = i // 2, i % 2
    s_next = (s + 1) % sections
    s_prev = (s + sections - 1) % sections
    t_right = (t + 1) % tensors
    t_left = (t + tensors - 1) % tensors
    t_far = (t + 2) % tensors

    w_copy = pltpu.make_async_copy(w_ref, wv, w_sem)
    w_copy.start()

    barrier = pltpu.get_barrier_semaphore()

    def greet(q, carry):
        pl.semaphore_signal(barrier, inc=1, device_id=(s_prev, q, t), device_id_type=MESH)
        return carry

    def greet_peer(q, carry):
        peer = (i + q) % REPL
        pl.semaphore_signal(barrier, inc=1, device_id=(s, peer, t), device_id_type=MESH)
        return carry

    lax.fori_loop(0, REPL, greet, 0)
    lax.fori_loop(1, REPL, greet_peer, 0)
    pl.semaphore_signal(barrier, inc=1, device_id=(s, i, t_right), device_id_type=MESH)
    pl.semaphore_signal(barrier, inc=1, device_id=(s, i, t_left), device_id_type=MESH)

    row_id = lax.broadcasted_iota(jnp.int32, (2 * HB, 2 * HB), 0)
    col_id = lax.broadcasted_iota(jnp.int32, (2 * HB, 2 * HB), 1)
    shared = row_id & col_id & (HB - 1)
    shared = shared ^ (shared >> 4)
    shared = shared ^ (shared >> 2)
    shared = shared ^ (shared >> 1)
    sign = (1 - 2 * (shared & 1)).astype(jnp.float32)
    signs = jnp.where((row_id // HB) == (col_id // HB), sign, 0.0).astype(jnp.bfloat16)

    def rotate(c):
        for part in range(FEAT // (2 * HB)):
            first = c * FEAT + part * 2 * HB
            block_rows = acts_ref[:, :, first:first + 2 * HB].reshape(NB * BLK, 2 * HB)
            turned = jnp.dot(block_rows, signs, preferred_element_type=jnp.float32)
            low = (turned * (1.0 / math.sqrt(HB))).astype(jnp.bfloat16)
            for piece in range(2):
                column = part * 2 * HB + piece * HB
                h, inside = column // HALF, column % HALF
                values = low[:, piece * HB:(piece + 1) * HB].reshape(NB, CHIPS, ROWS, HB)
                for l in range(NB):
                    sbuf[c, h, :, l, :, inside:inside + HB] = values[l]

    def spread(c):
        def send(e, carry):
            to_chip = rotated_chip(e // 2, chip)
            to_core = (e + 1 + core) % 2
            pltpu.make_async_remote_copy(
                src_ref=sbuf.at[c, to_core, to_chip],
                dst_ref=mid[c].at[i],
                send_sem=p1_send.at[c],
                recv_sem=p1_recv.at[c],
                device_id=(s_next, to_chip * 2 + to_core, t),
                device_id_type=MESH,
            ).start()
            return carry

        lax.fori_loop(0, REPL, send, 0)

    def pick(c, j, k):
        block = bs_ref[s * (REPL * NB) + j * NB + k]
        return mid[c][block % REPL, block // REPL]

    def deliver(c):
        pltpu.make_async_copy(mid[c], mid[c], p1_recv.at[c]).wait()

        def send(e, carry):
            to_chip = rotated_chip(e // 2, chip)
            to_core = (e + 1 + core) % 2
            j = to_chip * 2 + to_core
            for k in range(NB):
                obuf[c, j, k] = pick(c, j, k)
            pltpu.make_async_remote_copy(
                src_ref=obuf.at[c, j],
                dst_ref=x.at[t, c, core, :, chip],
                send_sem=p2_send.at[c],
                recv_sem=p2_recv.at[c],
                device_id=(s, j, t),
                device_id_type=MESH,
            ).start()
            return carry

        lax.fori_loop(0, REPL - 1, send, 0)
        for k in range(NB):
            x[t, c, core, k, chip] = pick(c, i, k)

    def y_copy(way, c):
        view = [x.at[t, c], x.at[t, c], x.at[t_left, c, 0], x.at[t_right, c, 1]][way]
        return pltpu.make_async_remote_copy(
            src_ref=view, dst_ref=view, send_sem=y_send.at[way, c], recv_sem=y_recv.at[way, c],
            device_id=(s, i, t_left if way % 2 else t_right), device_id_type=MESH)

    def gather_start(c):
        pltpu.make_async_copy(
            obuf.at[c, pl.ds(0, REPL - 1)], obuf.at[c, pl.ds(0, REPL - 1)], p2_recv.at[c]).wait()
        y_copy(0, c).start()
        y_copy(1, c).start()

    def gather_forward(c):
        y_copy(0, c).wait_recv()
        y_copy(2, c).start()
        y_copy(1, c).wait_recv()
        y_copy(3, c).start()

    def gather_finish(c):
        y_copy(2, c).wait_recv()
        y_copy(3, c).wait_recv()

    def piece(u, c):
        halves = [x[u, c, h].reshape(NB * BLK, HALF) for h in range(2)]
        return jnp.concatenate(halves, axis=1)

    def multiply(pieces):
        rows_in = []
        for u, c in pieces:
            value = piece(u, c)
            rows_in.append(value)
            wide = value.astype(jnp.float32)
            wide = wide * wide
            total = wide[:, :HB]
            for g in range(1, FEAT // HB):
                total = total + wide[:, g * HB:(g + 1) * HB]
            squares[...] += total

        def tile(n, carry):
            columns = pl.ds(pl.multiple_of(n * 256, 256), 256)
            result = acc[:, columns]
            for (u, c), value in zip(pieces, rows_in):
                rows_w = pl.ds(pl.multiple_of(u * LOCAL + c * FEAT, FEAT), FEAT)
                result = result + jnp.dot(value, wv[rows_w, columns], preferred_element_type=jnp.float32)
            acc[:, columns] = result
            return carry

        lax.fori_loop(0, COLS // 256, tile, 0)

    rotate(0)
    pl.semaphore_wait(barrier, 2 * REPL + 1)
    spread(0)
    for c in range(1, CHUNKS):
        rotate(c)
        if c < AHEAD:
            spread(c)

    acc[...] = jnp.zeros_like(acc)
    squares[...] = jnp.zeros_like(squares)
    lane = lax.broadcasted_iota(jnp.int32, (BLK, HD), 1)
    row = lax.broadcasted_iota(jnp.int32, (BLK, HD), 0)
    steps_f = (lane % (HD // 2)).astype(jnp.float32)
    inv_freq = jnp.exp(-math.log(rope_theta) * 2.0 * steps_f / HD)
    for k in range(NB):
        block = bs_ref[s * (REPL * NB) + i * NB + k]
        _, position = slot_docs(bs_ref, len_ref, s, block, row)
        angles = position.astype(jnp.float32) * inv_freq
        sine = jnp.sin(angles)
        cos_t[k * BLK:(k + 1) * BLK] = jnp.cos(angles)
        sin_t[k * BLK:(k + 1) * BLK] = jnp.where(lane < HD // 2, -sine, sine)

    w_copy.wait()
    for c in range(CHUNKS + 3):
        if c < CHUNKS:
            deliver(c)
            if c + AHEAD < CHUNKS:
                spread(c + AHEAD)
        if 0 <= c - 1 < CHUNKS:
            gather_start(c - 1)
        if 0 <= c - 2 < CHUNKS:
            gather_forward(c - 2)
        pieces = []
        if 0 <= c - 2 < CHUNKS:
            pieces += [(t, c - 2), (t_left, c - 2), (t_right, c - 2)]
        if 0 <= c - 3 < CHUNKS - 1:
            gather_finish(c - 3)
            pieces += [(t_far, c - 3)]
        if c - 3 == CHUNKS - 1:
            gather_finish(c - 3)
            pieces += [(t_far, c - 3)]
        if pieces:
            multiply(pieces)

    mean = jnp.sum(squares[...], axis=1, keepdims=True) * (1.0 / D)
    scale = lax.rsqrt(mean + norm_eps)
    cosine = cos_t[...] * scale
    sine = sin_t[...] * scale
    for head in range(GQ + 1):
        values = acc[:, head * HD:(head + 1) * HD]
        swapped = pltpu.roll(values, HD // 2, 1)
        qkv_ref[:, head * HD:(head + 1) * HD] = (values * cosine + swapped * sine).astype(jnp.bfloat16)
    last = (GQ + 1) * HD
    qkv_ref[:, last:last + HD] = (acc[:, last:last + HD] * scale).astype(jnp.bfloat16)

    for c in range(CHUNKS):
        pltpu.make_async_copy(sbuf.at[c], sbuf.at[c], p1_send.at[c]).wait()
        pltpu.make_async_copy(
            obuf.at[c, pl.ds(0, REPL - 1)], obuf.at[c, pl.ds(0, REPL - 1)], p2_send.at[c]).wait()
        for way in range(4):
            y_copy(way, c).wait_send()


def attention_kernel(qkv_ref, len_ref, bs_ref, out_ref, bias):
    s = lax.axis_index("section")
    i = lax.axis_index("dp")
    blocks = [bs_ref[s * (REPL * NB) + i * NB + k] for k in range(NB)]
    across = lax.broadcasted_iota(jnp.int32, (1, BLK), 1)
    down = lax.broadcasted_iota(jnp.int32, (BLK, 1), 0)
    seen_by = [slot_docs(bs_ref, len_ref, s, block, across) for block in blocks]
    key_doc = jnp.concatenate([v[0] for v in seen_by], axis=1)
    key_pos = jnp.concatenate([v[1] for v in seen_by], axis=1)
    for k in range(NB):
        row_doc, row_pos = slot_docs(bs_ref, len_ref, s, blocks[k], down)
        seen = (row_doc == key_doc) & (key_pos <= row_pos)
        bias[k * BLK:(k + 1) * BLK] = jnp.where(seen, 0.0, -1e30)

    keys = qkv_ref[:, GQ * HD:(GQ + 1) * HD]
    values = qkv_ref[:, (GQ + 1) * HD:]
    factor = math.log2(math.e) / math.sqrt(HD)
    for head in range(GQ):
        for k in range(NB):
            rows = slice(k * BLK, (k + 1) * BLK)
            queries = qkv_ref[rows, head * HD:(head + 1) * HD]
            scores = lax.dot_general(
                queries, keys, (((1,), (1,)), ((), ())), preferred_element_type=jnp.float32)
            scores = scores + bias[rows]
            row_max = jnp.max(scores, axis=1, keepdims=True)
            probs = jnp.exp2((scores - row_max) * factor)
            totals = jnp.sum(probs, axis=1, keepdims=True)
            context = jnp.dot(probs.astype(jnp.bfloat16), values, preferred_element_type=jnp.float32)
            out_ref[rows, head * HD:(head + 1) * HD] = (context / totals).astype(jnp.bfloat16)


def local(sections, tensors, acts, w_qkv, lengths, block_source):
    rows = NB * BLK
    flat_lengths = lengths.reshape(-1)
    flat_source = block_source.reshape(-1)
    vmem = pl.BlockSpec(memory_space=pltpu.VMEM)
    smem = pl.BlockSpec(memory_space=pltpu.SMEM)
    qkv = pl.pallas_call(
        functools.partial(exchange_kernel, sections, tensors),
        out_shape=jax.ShapeDtypeStruct((rows, COLS), jnp.bfloat16),
        in_specs=[vmem, pl.BlockSpec(memory_space=pl.ANY), smem, smem],
        out_specs=vmem,
        scratch_shapes=[
            pltpu.VMEM((CHUNKS, 2, CHIPS, NB, ROWS, HALF), jnp.bfloat16),
            pltpu.VMEM((CHUNKS, REPL, NB, ROWS, HALF), jnp.bfloat16),
            pltpu.VMEM((4, CHUNKS, 2, NB, CHIPS, ROWS, HALF), jnp.bfloat16),
            pltpu.VMEM((D, COLS), jnp.bfloat16),
            pltpu.VMEM((rows, COLS), jnp.float32),
            pltpu.VMEM((rows, HB), jnp.float32),
            pltpu.VMEM((rows, HD), jnp.float32),
            pltpu.VMEM((rows, HD), jnp.float32),
            pltpu.SemaphoreType.DMA,
            pltpu.SemaphoreType.DMA((CHUNKS,)),
            pltpu.SemaphoreType.DMA((CHUNKS,)),
            pltpu.SemaphoreType.DMA((CHUNKS,)),
            pltpu.SemaphoreType.DMA((CHUNKS,)),
            pltpu.SemaphoreType.DMA((4, CHUNKS)),
            pltpu.SemaphoreType.DMA((4, CHUNKS)),
        ] + [pltpu.VMEM((REPL, NB, ROWS, HALF), jnp.bfloat16)] * CHUNKS,
        compiler_params=pltpu.CompilerParams(
            collective_id=0, has_side_effects=True, vmem_limit_bytes=48 * 1024 * 1024),
        cost_estimate=pl.CostEstimate(
            flops=2 * rows * D * COLS, bytes_accessed=D * COLS * 2 + rows * COLS * 4, transcendentals=0),
    )(acts[0, :, 0], w_qkv[0], flat_lengths, flat_source)
    context = pl.pallas_call(
        attention_kernel,
        out_shape=jax.ShapeDtypeStruct((rows, GQ * HD), jnp.bfloat16),
        in_specs=[vmem, smem, smem],
        out_specs=vmem,
        scratch_shapes=[pltpu.VMEM((rows, rows), jnp.float32)],
        compiler_params=pltpu.CompilerParams(vmem_limit_bytes=32 * 1024 * 1024),
        cost_estimate=pl.CostEstimate(
            flops=4 * GQ * rows * rows * HD, bytes_accessed=rows * COLS * 4, transcendentals=GQ * rows * rows),
    )(qkv, flat_lengths, flat_source)
    return context[None]


def solution(mesh):
    placed = (P("section", None, "dp", None, "tensor"), P("section", None, "tensor"), P(), P())
    return jax.shard_map(
        functools.partial(local, mesh.shape["section"], mesh.shape["tensor"]),
        mesh=mesh, in_specs=placed, out_specs=P("section", "dp", "tensor"), check_vma=False,
    )
```

time: 220 us -> 90.4 us (0.41)
  waiting for transfers between devices: 152 us -> 0 us
  Pallas kernels: 0 us -> 85.9 us
  local copies, waits for them, and re-layouts: 28 us -> 2.88 us
  matrix products: 14.5 us -> 0 us
  between operations: 13.6 us -> 0.02 us
  other arithmetic: 8.31 us -> 0 us
    all_gather x2 -> x0, waiting for transfers between devices: 127 us -> none  [the longest x1 96.2 us: reassign(): gathered = lax.all_gather(own_blocks[None], 'dp', axis=0, tiled=True)]
    pallas_call x0 -> x2, Pallas kernels: none -> 85.9 us  [the longest x1 75.9 us: local(): pl.pallas_call(functools.partial(exchange_kernel, sections, tensors), out...]
    ppermute x1 -> x0, waiting for transfers between devices: 24.6 us -> none  [shifted(): return lax.ppermute(value, axis, pairs)]
    unnamed x6 -> x3, local copies, waits for them, and re-layouts: 16.9 us -> 2.01 us
    dot_general x4 -> x0, matrix products: 14.5 us -> none  [the longest x1 9.76 us: local(): projected = jnp.dot(normed, weight_cols, preferred_element_type=jnp.float32)]
    gather x2 -> x0, local copies, waits for them, and re-layouts: 8.39 us -> none  [the longest x1 7.35 us: reassign(): picked = gathered[block_owner[my_replica], block_slot[my_replica]]]
    reduce_sum x4 -> x0, other arithmetic: 5.29 us -> none  [the longest x1 3.08 us: local(): square_mean = jnp.mean(widened * widened, axis=-1, keepdims=True)]
  transfers between devices with their start and end apart: 3 -> 0, of which waited for: 3 -> 0; matrix products, arithmetic and copies ran while one was open for 9% -> 0% of each run, Pallas kernels for 0% -> 0%
where the time goes in v1:
time: 90.4 us; the launch traced here: 88.8 us
  Pallas kernels  85.9 us (95%)
  local copies, waits for them, and re-layouts  2.88 us (3%)
    pallas_call x1, Pallas kernels, local(): pl.pallas_call(functools.partial(exchange_kernel, sections, tensors), out...  75.9 us
    pallas_call x1, Pallas kernels, local(): pl.pallas_call(attention_kernel, out_shape=jax.ShapeDtypeStruct((rows, GQ...  10 us
    unnamed x3, local copies, waits for them, and re-layouts  2.01 us

profile of v1, /device:TPU:8, one launch (start us, length us, event | category | flops | bytes accessed | tf_op | source)
XLA Modules:
  0.0 88.8 jit_solution(11027427096238757245)
XLA Ops:
  0.0 0.8 reshape.7.bs_ref
  0.8 0.8 copy.5
  1.6 0.1 reshape.6.len_ref
  1.7 0.0 copy-start
  1.7 1.2 %copy-done = bf16[1,4,1,128,1024]{4,3,2,1,0:T(8,128)(2,1)S(1)} copy-done((bf16[1,4,1,128,1024]{4,3,2,1,0:T(8,128)(2,1)S(1)}, bf16[1,4,1,128,1024]{4,3,2,1,0:T(8,128)(2,1)}, u32[]{:S(2)}) %copy-start) | copy-done | bytes 1048600
  2.9 75.9 %shard_map.46.qkv_ref = bf16[512,1280]{1,0:T(8,128)(2,1)S(1)} custom-call(bf16[4,128,1024]{2,1,0:T(8,128)(2,1)S(1)} %bitcast.3, bf16[4096,1280]{1,0:T(8,128)(2,1)} %bitcast.4, s32[256]{0:T(256)S(1)} %reshape.6.len_ref, s32[256]{0:T(256)S(1)} %reshape.7.bs_ref), custom_call_target="tpu_custom_call" | custom-call | flops 5368709120 | bytes 13107200 | tf_op jit(solution)/shard_map/pallas_call | solution.py:304
  78.8 10.0 %shard_map.47 = bf16[512,1024]{1,0:T(8,128)(2,1)} custom-call(bf16[512,1280]{1,0:T(8,128)(2,1)S(1)} %shard_map.46.qkv_ref, s32[256]{0:T(256)S(1)} %reshape.6.len_ref, s32[256]{0:T(256)S(1)} %reshape.7.bs_ref), custom_call_target="tpu_custom_call" | custom-call | flops 1073741824 | bytes 2621440 | tf_op jit(solution)/shard_map/pallas_call | solution.py:331
Async XLA Ops:
  1.7 1.2 %copy-start = (bf16[1,4,1,128,1024]{4,3,2,1,0:T(8,128)(2,1)S(1)}, bf16[1,4,1,128,1024]{4,3,2,1,0:T(8,128)(2,1)}, u32[]{:S(2)}) copy-start(bf16[1,4,1,128,1024]{4,3,2,1,0:T(8,128)(2,1)} %param.4) | copy-start | bytes 3145732

commit v2 on v1

v2 whole, which is shorter than its diff:
```python
import functools
import math

import jax
import jax.numpy as jnp
from jax import lax
from jax.experimental import pallas as pl
from jax.experimental.pallas import tpu as pltpu
from jax.sharding import PartitionSpec as P

HD = 128
HB = 128
BLK = 128
DOCS = 4
TOK_DEV = 512
GQ = 8
NB = 4
D = 4096
LOCAL = 1024
COLS = 1280
CHIPS = 8
REPL = 16
CHUNKS = 4
FEAT = LOCAL // CHUNKS
HALF = FEAT // 2
ROWS = 16
AHEAD = 2
VMEM_BYTES = 48 * 1024 * 1024
GROUP = 8

norm_eps = 1e-05
rope_theta = 500000.0
MESH = pl.DeviceIdType.MESH


def far_first(step, chip, core):
    size = (step + 1) // 2
    offset = (1 - step % 2) * (CHIPS // 2 - size) - (step % 2) * (size % (CHIPS // 2))
    return (chip + CHIPS + (1 - 2 * core) * offset) % CHIPS


def near_first(step, chip, core):
    size = (step + 1) // 2
    offset = (2 * (step % 2) - 1) * size
    return (chip + CHIPS + (1 - 2 * core) * offset) % CHIPS


def slot_docs(bs_ref, len_ref, section, block, offset_iota):
    window = block // NB
    offset = (block % NB) * BLK + offset_iota
    end = len_ref[section, 0, window]
    start = jnp.zeros_like(offset)
    document = jnp.zeros_like(offset)
    for d in range(DOCS):
        past = offset >= end
        document = document + past.astype(jnp.int32)
        start = jnp.where(past, end, start)
        if d < DOCS - 1:
            end = end + len_ref[section, d + 1, window]
    return window * DOCS + document, offset - start


def exchange_kernel(
    sections, tensors, acts_ref, w_ref, len_ref, bs_ref, qkv_ref,
    rows_in, sbuf, obuf, x, wv, acc, squares, cos_t, sin_t,
    a_sem, w_sem, p1_send, p1_recv, p2_send, p2_recv, y_send, y_recv, *mid
):
    s = lax.axis_index("section")
    i = lax.axis_index("dp")
    t = lax.axis_index("tensor")
    chip, core = i // 2, i % 2
    s_next = (s + 1) % sections
    s_prev = (s + sections - 1) % sections
    t_right = (t + 1) % tensors
    t_left = (t + tensors - 1) % tensors
    t_far = (t + 2) % tensors

    def fetch(c):
        return pltpu.make_async_copy(
            acts_ref.at[:, :, pl.ds(c * FEAT, FEAT)], rows_in.at[c], a_sem.at[c])

    for c in range(CHUNKS):
        fetch(c).start()
    w_copy = pltpu.make_async_copy(w_ref, wv, w_sem)
    w_copy.start()

    barrier = pltpu.get_barrier_semaphore()

    def greet(q, carry):
        pl.semaphore_signal(barrier, inc=1, device_id=(s_prev, q, t), device_id_type=MESH)
        return carry

    def greet_peer(q, carry):
        peer = (i + q) % REPL
        pl.semaphore_signal(barrier, inc=1, device_id=(s, peer, t), device_id_type=MESH)
        return carry

    lax.fori_loop(0, REPL, greet, 0)
    lax.fori_loop(1, REPL, greet_peer, 0)
    pl.semaphore_signal(barrier, inc=1, device_id=(s, i, t_right), device_id_type=MESH)
    pl.semaphore_signal(barrier, inc=1, device_id=(s, i, t_left), device_id_type=MESH)

    row_id = lax.broadcasted_iota(jnp.int32, (2 * HB, 2 * HB), 0)
    col_id = lax.broadcasted_iota(jnp.int32, (2 * HB, 2 * HB), 1)
    shared = row_id & col_id & (HB - 1)
    shared = shared ^ (shared >> 4)
    shared = shared ^ (shared >> 2)
    shared = shared ^ (shared >> 1)
    sign = (1 - 2 * (shared & 1)).astype(jnp.float32)
    signs = jnp.where((row_id // HB) == (col_id // HB), sign, 0.0).astype(jnp.bfloat16)

    def rotate(c):
        fetch(c).wait()
        for part in range(FEAT // (2 * HB)):
            first = part * 2 * HB
            block_rows = rows_in[c, :, :, first:first + 2 * HB].reshape(NB * BLK, 2 * HB)
            turned = jnp.dot(block_rows, signs, preferred_element_type=jnp.float32)
            low = (turned * (1.0 / math.sqrt(HB))).astype(jnp.bfloat16)
            for piece in range(2):
                column = part * 2 * HB + piece * HB
                h, inside = column // HALF, column % HALF
                values = low[:, piece * HB:(piece + 1) * HB].reshape(NB, CHIPS, ROWS, HB)
                for l in range(NB):
                    sbuf[c, h, :, l, :, inside:inside + HB] = values[l]

    def spread(c):
        def send(e, carry):
            to_chip = far_first(e % CHIPS, chip, core)
            to_core = (e // CHIPS + 1 + core) % 2
            pltpu.make_async_remote_copy(
                src_ref=sbuf.at[c, to_core, to_chip],
                dst_ref=mid[c].at[i],
                send_sem=p1_send.at[c],
                recv_sem=p1_recv.at[c],
                device_id=(s_next, to_chip * 2 + to_core, t),
                device_id_type=MESH,
            ).start()
            return carry

        lax.fori_loop(0, REPL, send, 0)

    def pick(c, j, k):
        block = bs_ref[s, j * NB + k]
        return mid[c][block % REPL, block // REPL]

    def deliver(c):
        pltpu.make_async_copy(mid[c], mid[c], p1_recv.at[c]).wait()

        def send(e, carry):
            to_chip = near_first(e // 2, chip, core)
            to_core = (e + core) % 2
            j = to_chip * 2 + to_core
            for k in range(NB):
                obuf[c, j, k] = pick(c, j, k)
            pltpu.make_async_remote_copy(
                src_ref=obuf.at[c, j],
                dst_ref=x.at[t, c, core, :, chip],
                send_sem=p2_send.at[c],
                recv_sem=p2_recv.at[c],
                device_id=(s, j, t),
                device_id_type=MESH,
            ).start()
            return carry

        lax.fori_loop(1, REPL, send, 0)
        for k in range(NB):
            x[t, c, core, k, chip] = pick(c, i, k)

    def y_copy(way, c):
        to_left, turn = way % 2, way // 2
        owner = t if turn < 2 else (t_right if to_left else t_left)
        half = (turn + to_left) % 2
        view = x.at[owner, c, half]
        return pltpu.make_async_remote_copy(
            src_ref=view, dst_ref=view, send_sem=y_send.at[way, c], recv_sem=y_recv.at[way, c],
            device_id=(s, i, t_left if to_left else t_right), device_id_type=MESH)

    def gather_start(c):
        pltpu.make_async_copy(
            obuf.at[c, pl.ds(0, REPL - 1)], obuf.at[c, pl.ds(0, REPL - 1)], p2_recv.at[c]).wait()
        for way in range(4):
            y_copy(way, c).start()

    def gather_forward(c):
        for way in range(2):
            y_copy(way, c).wait_recv()
            y_copy(way + 4, c).start()

    def gather_near(c):
        for way in range(2, 4):
            y_copy(way, c).wait_recv()

    def gather_finish(c):
        for way in range(4, 6):
            y_copy(way, c).wait_recv()

    def piece(u, c):
        halves = [x[u, c, h].reshape(NB * BLK, HALF) for h in range(2)]
        return jnp.concatenate(halves, axis=1)

    def multiply(pieces):
        rows_in = []
        for u, c in pieces:
            value = piece(u, c)
            rows_in.append(value)
            wide = value.astype(jnp.float32)
            wide = wide * wide
            total = wide[:, :HB]
            for g in range(1, FEAT // HB):
                total = total + wide[:, g * HB:(g + 1) * HB]
            squares[...] += total

        def tile(n, carry):
            columns = pl.ds(pl.multiple_of(n * 256, 256), 256)
            result = acc[:, columns]
            for (u, c), value in zip(pieces, rows_in):
                rows_w = pl.ds(pl.multiple_of(u * LOCAL + c * FEAT, FEAT), FEAT)
                result = result + jnp.dot(value, wv[rows_w, columns], preferred_element_type=jnp.float32)
            acc[:, columns] = result
            return carry

        lax.fori_loop(0, COLS // 256, tile, 0)

    rotate(0)
    pl.semaphore_wait(barrier, 2 * REPL + 1)
    spread(0)
    for c in range(1, CHUNKS):
        rotate(c)
        if c < AHEAD:
            spread(c)

    acc[...] = jnp.zeros_like(acc)
    squares[...] = jnp.zeros_like(squares)
    lane = lax.broadcasted_iota(jnp.int32, (BLK, HD), 1)
    row = lax.broadcasted_iota(jnp.int32, (BLK, HD), 0)
    steps_f = (lane % (HD // 2)).astype(jnp.float32)
    inv_freq = jnp.exp(-math.log(rope_theta) * 2.0 * steps_f / HD)
    for k in range(NB):
        block = bs_ref[s, i * NB + k]
        _, position = slot_docs(bs_ref, len_ref, s, block, row)
        angles = position.astype(jnp.float32) * inv_freq
        sine = jnp.sin(angles)
        cos_t[k * BLK:(k + 1) * BLK] = jnp.cos(angles)
        sin_t[k * BLK:(k + 1) * BLK] = jnp.where(lane < HD // 2, -sine, sine)

    w_copy.wait()
    for c in range(CHUNKS + 2):
        if c < CHUNKS:
            deliver(c)
            if c + AHEAD < CHUNKS:
                spread(c + AHEAD)
        if c >= 2:
            gather_forward(c - 2)
            gather_near(c - 2)
            multiply([(t, c - 2), (t_left, c - 2), (t_right, c - 2)])
            gather_finish(c - 2)
            multiply([(t_far, c - 2)])
        if 0 <= c - 1 < CHUNKS:
            gather_start(c - 1)

    mean = jnp.sum(squares[...], axis=1, keepdims=True) * (1.0 / D)
    scale = lax.rsqrt(mean + norm_eps)
    cosine = cos_t[...] * scale
    sine = sin_t[...] * scale
    for head in range(GQ + 1):
        values = acc[:, head * HD:(head + 1) * HD]
        swapped = pltpu.roll(values, HD // 2, 1)
        qkv_ref[:, head * HD:(head + 1) * HD] = (values * cosine + swapped * sine).astype(jnp.bfloat16)
    last = (GQ + 1) * HD
    qkv_ref[:, last:last + HD] = (acc[:, last:last + HD] * scale).astype(jnp.bfloat16)

    for c in range(CHUNKS):
        pltpu.make_async_copy(sbuf.at[c], sbuf.at[c], p1_send.at[c]).wait()
        pltpu.make_async_copy(
            obuf.at[c, pl.ds(0, REPL - 1)], obuf.at[c, pl.ds(0, REPL - 1)], p2_send.at[c]).wait()
        for way in range(6):
            y_copy(way, c).wait_send()


def attention_kernel(qkv_ref, len_ref, bs_ref, out_ref, keys, values, context, out_sem):
    s = lax.axis_index("section")
    i = lax.axis_index("dp")
    blocks = [bs_ref[s, i * NB + k] for k in range(NB)]
    ranks = [sum((other < block).astype(jnp.int32) for other in blocks) for block in blocks]
    slots = [sum(k * (ranks[k] == r).astype(jnp.int32) for k in range(NB)) for r in range(NB)]
    ordered = [sum(blocks[k] * (ranks[k] == r).astype(jnp.int32) for k in range(NB)) for r in range(NB)]
    across = lax.broadcasted_iota(jnp.int32, (1, BLK), 1)
    down = lax.broadcasted_iota(jnp.int32, (BLK, 1), 0)
    key_docs = [slot_docs(bs_ref, len_ref, s, block, across) for block in ordered]
    slot_rows = [pl.ds(pl.multiple_of(slot * BLK, BLK), BLK) for slot in slots]
    for r in range(NB):
        keys[:, r * BLK:(r + 1) * BLK] = qkv_ref[slot_rows[r], GQ * HD:(GQ + 1) * HD].T
        values[r * BLK:(r + 1) * BLK] = qkv_ref[slot_rows[r], (GQ + 1) * HD:]
    factor = math.log2(math.e) / math.sqrt(HD)

    def attend(r, first):
        row_doc, row_pos = slot_docs(bs_ref, len_ref, s, ordered[r], down)
        key_doc = jnp.concatenate([key_docs[f][0] for f in range(first, r + 1)], axis=1)
        key_pos = jnp.concatenate([key_docs[f][1] for f in range(first, r + 1)], axis=1)
        seen = (row_doc == key_doc) & (key_pos <= row_pos)
        near = slice(first * BLK, (r + 1) * BLK)
        near_keys, near_values = keys[:, near], values[near]
        for head in range(0, GQ, GROUP):
            group = range(head, head + GROUP)
            scores = [
                jnp.dot(qkv_ref[slot_rows[r], h * HD:(h + 1) * HD], near_keys, preferred_element_type=jnp.float32)
                for h in group
            ]
            scores = [jnp.where(seen, value, -1e30) for value in scores]
            row_max = [jnp.max(value, axis=1, keepdims=True) for value in scores]
            probs = [jnp.exp2((value - top) * factor) for value, top in zip(scores, row_max)]
            totals = [jnp.sum(value, axis=1, keepdims=True) for value in probs]
            sums = [
                jnp.dot(value.astype(jnp.bfloat16), near_values, preferred_element_type=jnp.float32)
                for value in probs
            ]
            for h, value, total in zip(group, sums, totals):
                context[r, :, h * HD:(h + 1) * HD] = (value / total).astype(jnp.bfloat16)

    copies = []
    for r in range(NB):
        same = [(ordered[f] // NB == ordered[r] // NB).astype(jnp.int32) for f in range(r)]
        count = sum(same) if same else jnp.int32(0)
        for earlier in range(r + 1):
            pl.when(count == earlier)(functools.partial(attend, r, r - earlier))
        copies.append(pltpu.make_async_copy(context.at[r], out_ref.at[slot_rows[r]], out_sem.at[r]))
        copies[r].start()
    for copy in copies:
        copy.wait()


def attention(qkv, by_document, block_source):
    rows = NB * BLK
    vmem = pl.BlockSpec(memory_space=pltpu.VMEM)
    smem = pl.BlockSpec(memory_space=pltpu.SMEM)
    return pl.pallas_call(
        attention_kernel,
        out_shape=jax.ShapeDtypeStruct((rows, GQ * HD), jnp.bfloat16),
        in_specs=[vmem, smem, smem],
        out_specs=pl.BlockSpec(memory_space=pl.ANY),
        scratch_shapes=[
            pltpu.VMEM((HD, rows), jnp.bfloat16),
            pltpu.VMEM((rows, HD), jnp.bfloat16),
            pltpu.VMEM((NB, BLK, GQ * HD), jnp.bfloat16),
            pltpu.SemaphoreType.DMA((NB,)),
        ],
        compiler_params=pltpu.CompilerParams(vmem_limit_bytes=32 * 1024 * 1024),
        cost_estimate=pl.CostEstimate(
            flops=4 * GQ * rows * rows * HD, bytes_accessed=rows * COLS * 4, transcendentals=GQ * rows * rows),
    )(qkv, by_document, block_source)


def local(sections, tensors, acts, w_qkv, lengths, block_source):
    rows = NB * BLK
    by_document = lengths.transpose(0, 2, 1)
    vmem = pl.BlockSpec(memory_space=pltpu.VMEM)
    smem = pl.BlockSpec(memory_space=pltpu.SMEM)
    qkv = pl.pallas_call(
        functools.partial(exchange_kernel, sections, tensors),
        out_shape=jax.ShapeDtypeStruct((rows, COLS), jnp.bfloat16),
        in_specs=[pl.BlockSpec(memory_space=pltpu.HBM)] * 2 + [smem] * 2,
        out_specs=vmem,
        scratch_shapes=[
            pltpu.VMEM((CHUNKS, NB, BLK, FEAT), jnp.bfloat16),
            pltpu.VMEM((CHUNKS, 2, CHIPS, NB, ROWS, HALF), jnp.bfloat16),
            pltpu.VMEM((CHUNKS, REPL, NB, ROWS, HALF), jnp.bfloat16),
            pltpu.VMEM((4, CHUNKS, 2, NB, CHIPS, ROWS, HALF), jnp.bfloat16),
            pltpu.VMEM((D, COLS), jnp.bfloat16),
            pltpu.VMEM((rows, COLS), jnp.float32),
            pltpu.VMEM((rows, HB), jnp.float32),
            pltpu.VMEM((rows, HD), jnp.float32),
            pltpu.VMEM((rows, HD), jnp.float32),
            pltpu.SemaphoreType.DMA((CHUNKS,)),
            pltpu.SemaphoreType.DMA,
            pltpu.SemaphoreType.DMA((CHUNKS,)),
            pltpu.SemaphoreType.DMA((CHUNKS,)),
            pltpu.SemaphoreType.DMA((CHUNKS,)),
            pltpu.SemaphoreType.DMA((CHUNKS,)),
            pltpu.SemaphoreType.DMA((6, CHUNKS)),
            pltpu.SemaphoreType.DMA((6, CHUNKS)),
        ] + [pltpu.VMEM((REPL, NB, ROWS, HALF), jnp.bfloat16)] * CHUNKS,
        compiler_params=pltpu.CompilerParams(
            collective_id=0, has_side_effects=True, vmem_limit_bytes=VMEM_BYTES),
        cost_estimate=pl.CostEstimate(
            flops=2 * rows * D * COLS, bytes_accessed=D * COLS * 2 + rows * COLS * 4, transcendentals=0),
    )(acts[0, :, 0], w_qkv[0], by_document, block_source)
    return attention(qkv, by_document, block_source)[None]


def solution(mesh):
    placed = (P("section", None, "dp", None, "tensor"), P("section", None, "tensor"), P(), P())
    return jax.shard_map(
        functools.partial(local, mesh.shape["section"], mesh.shape["tensor"]),
        mesh=mesh, in_specs=placed, out_specs=P("section", "dp", "tensor"), check_vma=False,
    )
```

time: 90.4 us -> 85.8 us (0.949); the launches traced: 88.8 us -> 85.6 us
  Pallas kernels: 85.9 us -> 83 us
    pallas_call x1, Pallas kernels: 10 us -> 3.72 us  [attention(): pl.pallas_call(attention_kernel, out_shape=jax.ShapeDtypeStruct((rows, GQ...]
    pallas_call x1, Pallas kernels: 75.9 us -> 79.3 us  [local(): pl.pallas_call(functools.partial(exchange_kernel, sections, tensors), out...]
    unnamed x3 -> x6, local copies, waits for them, and re-layouts: 2.01 us -> 2.6 us
where the time goes in v2:
time: 85.8 us; the launch traced here: 85.6 us
  Pallas kernels  83 us (97%)
  local copies, waits for them, and re-layouts  2.6 us (3%)
    pallas_call x1, Pallas kernels, local(): pl.pallas_call(functools.partial(exchange_kernel, sections, tensors), out...  79.3 us
    pallas_call x1, Pallas kernels, attention(): pl.pallas_call(attention_kernel, out_shape=jax.ShapeDtypeStruct((rows, GQ...  3.72 us
    unnamed x6, local copies, waits for them, and re-layouts  2.6 us

profile of v2, /device:TPU:8, one launch (start us, length us, event | category | flops | bytes accessed | tf_op | source)
XLA Modules:
  0.0 85.6 jit_solution(6328222836487186259)
XLA Ops:
  0.0 0.0 copy-start
  0.0 1.2 %copy-done = bf16[1,4,1,128,1024]{4,3,2,1,0:T(8,128)(2,1)S(1)} copy-done((bf16[1,4,1,128,1024]{4,3,2,1,0:T(8,128)(2,1)S(1)}, bf16[1,4,1,128,1024]{4,3,2,1,0:T(8,128)(2,1)}, u32[]{:S(2)}) %copy-start) | copy-done | bytes 1048600
  1.2 0.0 copy-start.1
  1.2 0.7 copy-done.1
  1.9 0.0 copy-start.2
  1.9 0.7 copy-done.2
  2.6 79.3 %shard_map.46.qkv_ref = bf16[512,1280]{1,0:T(8,128)(2,1)S(1)} custom-call(bf16[4,128,1024]{2,1,0:T(8,128)(2,1)S(1)} %bitcast.4, bf16[4096,1280]{1,0:T(8,128)(2,1)} %bitcast.7, s32[4,4,16]{2,1,0:T(4,128)S(1)} %bitcast.5, s32[4,64]{1,0:T(4,128)S(1)} %copy-done.2), custom_call_target="tpu_custom_call" | custom-call | flops 5368709120 | bytes 13107200 | tf_op jit(solution)/shard_map/pallas_call | solution.py:358
  81.9 3.7 %shard_map.47 = bf16[512,1024]{1,0:T(8,128)(2,1)} custom-call(bf16[512,1280]{1,0:T(8,128)(2,1)S(1)} %shard_map.46.qkv_ref, s32[4,4,16]{2,1,0:T(4,128)S(1)} %bitcast.6, s32[4,64]{1,0:T(4,128)S(1)} %copy-done.2), custom_call_target="tpu_custom_call" | custom-call | flops 1073741824 | bytes 2621440 | tf_op jit(solution)/shard_map/pallas_call | solution.py:336
Async XLA Ops:
  0.0 1.2 %copy-start = (bf16[1,4,1,128,1024]{4,3,2,1,0:T(8,128)(2,1)S(1)}, bf16[1,4,1,128,1024]{4,3,2,1,0:T(8,128)(2,1)}, u32[]{:S(2)}) copy-start(bf16[1,4,1,128,1024]{4,3,2,1,0:T(8,128)(2,1)} %param.4) | copy-start | bytes 3145732
  1.2 0.7 copy-start.1
  1.9 0.7 copy-start.2

commit v3 on v2

--- a/solution.py
+++ b/solution.py
@@ -25,6 +25,9 @@
 HALF = FEAT // 2
 ROWS = 16
 AHEAD = 2
+EARLY = 1
+SPLIT = 1
+SLOTS = NB // SPLIT
 VMEM_BYTES = 48 * 1024 * 1024
 GROUP = 8
 
@@ -36,12 +39,6 @@
 def far_first(step, chip, core):
     size = (step + 1) // 2
     offset = (1 - step % 2) * (CHIPS // 2 - size) - (step % 2) * (size % (CHIPS // 2))
-    return (chip + CHIPS + (1 - 2 * core) * offset) % CHIPS
-
-
-def near_first(step, chip, core):
-    size = (step + 1) // 2
-    offset = (2 * (step % 2) - 1) * size
     return (chip + CHIPS + (1 - 2 * core) * offset) % CHIPS
 
 
@@ -146,80 +143,110 @@
     def deliver(c):
         pltpu.make_async_copy(mid[c], mid[c], p1_recv.at[c]).wait()
 
-        def send(e, carry):
-            to_chip = near_first(e // 2, chip, core)
-            to_core = (e + core) % 2
-            j = to_chip * 2 + to_core
-            for k in range(NB):
-                obuf[c, j, k] = pick(c, j, k)
-            pltpu.make_async_remote_copy(
-                src_ref=obuf.at[c, j],
-                dst_ref=x.at[t, c, core, :, chip],
-                send_sem=p2_send.at[c],
-                recv_sem=p2_recv.at[c],
-                device_id=(s, j, t),
-                device_id_type=MESH,
-            ).start()
-            return carry
-
-        lax.fori_loop(1, REPL, send, 0)
-        for k in range(NB):
-            x[t, c, core, k, chip] = pick(c, i, k)
-
-    def y_copy(way, c):
+        for part in range(SPLIT):
+            slots = range(part * SLOTS, (part + 1) * SLOTS)
+
+            def send(e, carry):
+                to_chip = far_first((e - 1) % CHIPS, chip, core)
+                to_core = ((e - 1) // CHIPS + 1 + core) % 2
+                j = to_chip * 2 + to_core
+                for k in slots:
+                    obuf[c, part, j, k % SLOTS] = pick(c, j, k)
+                pltpu.make_async_remote_copy(
+                    src_ref=obuf.at[c, part, j],
+                    dst_ref=x.at[t, c, part, core, chip],
+                    send_sem=p2_send.at[c, part],
+                    recv_sem=p2_recv.at[c, part],
+                    device_id=(s, j, t),
+                    device_id_type=MESH,
+                ).start()
+                return carry
+
+            lax.fori_loop(1, REPL, send, 0)
+            for k in slots:
+                x[t, c, part, core, chip, k % SLOTS] = pick(c, i, k)
+
+    def delivered(c, part, sem):
+        view = obuf.at[c, part, pl.ds(0, REPL - 1)]
+        return pltpu.make_async_copy(view, view, sem.at[c, part])
+
+    def y_copy(way, c, part):
         to_left, turn = way % 2, way // 2
         owner = t if turn < 2 else (t_right if to_left else t_left)
         half = (turn + to_left) % 2
-        view = x.at[owner, c, half]
+        view = x.at[owner, c, part, half]
         return pltpu.make_async_remote_copy(
-            src_ref=view, dst_ref=view, send_sem=y_send.at[way, c], recv_sem=y_recv.at[way, c],
+            src_ref=view, dst_ref=view, send_sem=y_send.at[way, c, part], recv_sem=y_recv.at[way, c, part],
             device_id=(s, i, t_left if to_left else t_right), device_id_type=MESH)
 
-    def gather_start(c):
-        pltpu.make_async_copy(
-            obuf.at[c, pl.ds(0, REPL - 1)], obuf.at[c, pl.ds(0, REPL - 1)], p2_recv.at[c]).wait()
+    def gather_start(c, part):
+        delivered(c, part, p2_recv).wait()
         for way in range(4):
-            y_copy(way, c).start()
-
-    def gather_forward(c):
+            y_copy(way, c, part).start()
+
+    def gather_forward(c, part):
         for way in range(2):
-            y_copy(way, c).wait_recv()
-            y_copy(way + 4, c).start()
-
-    def gather_near(c):
+            y_copy(way, c, part).wait_recv()
+            y_copy(way + 4, c, part).start()
+
+    def gather_near(c, part):
         for way in range(2, 4):
-            y_copy(way, c).wait_recv()
-
-    def gather_finish(c):
+            y_copy(way, c, part).wait_recv()
+
+    def gather_far(c, part):
         for way in range(4, 6):
-            y_copy(way, c).wait_recv()
-
-    def piece(u, c):
-        halves = [x[u, c, h].reshape(NB * BLK, HALF) for h in range(2)]
+            y_copy(way, c, part).wait_recv()
+
+    def piece(u, c, part):
+        halves = [x[u, c, part, h].reshape(SLOTS * BLK, HALF) for h in range(2)]
         return jnp.concatenate(halves, axis=1)
 
-    def multiply(pieces):
-        rows_in = []
-        for u, c in pieces:
-            value = piece(u, c)
-            rows_in.append(value)
+    def multiply(c, part, owners):
+        rows = pl.ds(part * SLOTS * BLK, SLOTS * BLK)
+        pieces = [piece(u, c, part) for u in owners]
+        for value in pieces:
             wide = value.astype(jnp.float32)
             wide = wide * wide
             total = wide[:, :HB]
             for g in range(1, FEAT // HB):
                 total = total + wide[:, g * HB:(g + 1) * HB]
-            squares[...] += total
+            squares[rows] += total
 
         def tile(n, carry):
             columns = pl.ds(pl.multiple_of(n * 256, 256), 256)
-            result = acc[:, columns]
-            for (u, c), value in zip(pieces, rows_in):
+            result = acc[rows, columns]
+            for u, value in zip(owners, pieces):
                 rows_w = pl.ds(pl.multiple_of(u * LOCAL + c * FEAT, FEAT), FEAT)
                 result = result + jnp.dot(value, wv[rows_w, columns], preferred_element_type=jnp.float32)
-            acc[:, columns] = result
+            acc[rows, columns] = result
             return carry
 
         lax.fori_loop(0, COLS // 256, tile, 0)
+
+    def project(c, part):
+        gather_near(c, part)
+        gather_far(c, part)
+        multiply(c, part, [t, t_left, t_right, t_far])
+
+    def finish(part):
+        rows = pl.ds(part * SLOTS * BLK, SLOTS * BLK)
+        mean = jnp.sum(squares[rows], axis=1, keepdims=True) * (1.0 / D)
+        scale = lax.rsqrt(mean + norm_eps)
+        cosine = cos_t[part].reshape(SLOTS * BLK, HD) * scale
+        sine = sin_t[part].reshape(SLOTS * BLK, HD) * scale
+
+        def put(head, result):
+            low = result.astype(jnp.bfloat16).reshape(CHIPS, SLOTS, ROWS, HD)
+            for k in range(SLOTS):
+                first = (part * SLOTS + k) * BLK
+                qkv_ref[first:first + BLK, head * HD:(head + 1) * HD] = low[:, k].reshape(BLK, HD)
+
+        for head in range(GQ + 1):
+            values = acc[rows, head * HD:(head + 1) * HD]
+            swapped = pltpu.roll(values, HD // 2, 1)
+            put(head, values * cosine + swapped * sine)
+        last = (GQ + 1) * HD
+        put(GQ + 1, acc[rows, last:last + HD] * scale)
 
     rotate(0)
     pl.semaphore_wait(barrier, 2 * REPL + 1)
@@ -240,41 +267,43 @@
         _, position = slot_docs(bs_ref, len_ref, s, block, row)
         angles = position.astype(jnp.float32) * inv_freq
         sine = jnp.sin(angles)
-        cos_t[k * BLK:(k + 1) * BLK] = jnp.cos(angles)
-        sin_t[k * BLK:(k + 1) * BLK] = jnp.where(lane < HD // 2, -sine, sine)
+        sine = jnp.where(lane < HD // 2, -sine, sine)
+        cos_t[k // SLOTS, :, k % SLOTS] = jnp.cos(angles).reshape(CHIPS, ROWS, HD)
+        sin_t[k // SLOTS, :, k % SLOTS] = sine.reshape(CHIPS, ROWS, HD)
 
     w_copy.wait()
-    for c in range(CHUNKS + 2):
-        if c < CHUNKS:
-            deliver(c)
-            if c + AHEAD < CHUNKS:
-                spread(c + AHEAD)
-        if c >= 2:
-            gather_forward(c - 2)
-            gather_near(c - 2)
-            multiply([(t, c - 2), (t_left, c - 2), (t_right, c - 2)])
-            gather_finish(c - 2)
-            multiply([(t_far, c - 2)])
-        if 0 <= c - 1 < CHUNKS:
-            gather_start(c - 1)
-
-    mean = jnp.sum(squares[...], axis=1, keepdims=True) * (1.0 / D)
-    scale = lax.rsqrt(mean + norm_eps)
-    cosine = cos_t[...] * scale
-    sine = sin_t[...] * scale
-    for head in range(GQ + 1):
-        values = acc[:, head * HD:(head + 1) * HD]
-        swapped = pltpu.roll(values, HD // 2, 1)
-        qkv_ref[:, head * HD:(head + 1) * HD] = (values * cosine + swapped * sine).astype(jnp.bfloat16)
-    last = (GQ + 1) * HD
-    qkv_ref[:, last:last + HD] = (acc[:, last:last + HD] * scale).astype(jnp.bfloat16)
+    for c in range(AHEAD):
+        deliver(c)
+        spread(c + AHEAD)
+    waiting = []
+    for c in range(CHUNKS):
+        for part in range(SPLIT):
+            gather_start(c, part)
+            if c >= CHUNKS - AHEAD and len(waiting) > 1:
+                project(*waiting.pop(0))
+            gather_forward(c, part)
+            waiting.append((c, part))
+        if c + AHEAD < CHUNKS:
+            deliver(c + AHEAD)
+            while len(waiting) > EARLY:
+                project(*waiting.pop(0))
+    while len(waiting) > 1:
+        project(*waiting.pop(0))
+    for part in range(SPLIT - 1):
+        finish(part)
+    c, part = waiting[0]
+    gather_near(c, part)
+    multiply(c, part, [t, t_left, t_right])
+    gather_far(c, part)
+    multiply(c, part, [t_far])
+    finish(part)
 
     for c in range(CHUNKS):
         pltpu.make_async_copy(sbuf.at[c], sbuf.at[c], p1_send.at[c]).wait()
-        pltpu.make_async_copy(
-            obuf.at[c, pl.ds(0, REPL - 1)], obuf.at[c, pl.ds(0, REPL - 1)], p2_send.at[c]).wait()
-        for way in range(6):
-            y_copy(way, c).wait_send()
+        for part in range(SPLIT):
+            delivered(c, part, p2_send).wait()
+            for way in range(6):
+                y_copy(way, c, part).wait_send()
 
 
 def attention_kernel(qkv_ref, len_ref, bs_ref, out_ref, keys, values, context, out_sem):
@@ -363,21 +392,21 @@
         scratch_shapes=[
             pltpu.VMEM((CHUNKS, NB, BLK, FEAT), jnp.bfloat16),
             pltpu.VMEM((CHUNKS, 2, CHIPS, NB, ROWS, HALF), jnp.bfloat16),
-            pltpu.VMEM((CHUNKS, REPL, NB, ROWS, HALF), jnp.bfloat16),
-            pltpu.VMEM((4, CHUNKS, 2, NB, CHIPS, ROWS, HALF), jnp.bfloat16),
+            pltpu.VMEM((CHUNKS, SPLIT, REPL, SLOTS, ROWS, HALF), jnp.bfloat16),
+            pltpu.VMEM((4, CHUNKS, SPLIT, 2, CHIPS, SLOTS, ROWS, HALF), jnp.bfloat16),
             pltpu.VMEM((D, COLS), jnp.bfloat16),
             pltpu.VMEM((rows, COLS), jnp.float32),
             pltpu.VMEM((rows, HB), jnp.float32),
-            pltpu.VMEM((rows, HD), jnp.float32),
-            pltpu.VMEM((rows, HD), jnp.float32),
+            pltpu.VMEM((SPLIT, CHIPS, SLOTS, ROWS, HD), jnp.float32),
+            pltpu.VMEM((SPLIT, CHIPS, SLOTS, ROWS, HD), jnp.float32),
             pltpu.SemaphoreType.DMA((CHUNKS,)),
             pltpu.SemaphoreType.DMA,
             pltpu.SemaphoreType.DMA((CHUNKS,)),
             pltpu.SemaphoreType.DMA((CHUNKS,)),
-            pltpu.SemaphoreType.DMA((CHUNKS,)),
-            pltpu.SemaphoreType.DMA((CHUNKS,)),
-            pltpu.SemaphoreType.DMA((6, CHUNKS)),
-            pltpu.SemaphoreType.DMA((6, CHUNKS)),
+            pltpu.SemaphoreType.DMA((CHUNKS, SPLIT)),
+            pltpu.SemaphoreType.DMA((CHUNKS, SPLIT)),
+            pltpu.SemaphoreType.DMA((6, CHUNKS, SPLIT)),
+            pltpu.SemaphoreType.DMA((6, CHUNKS, SPLIT)),
         ] + [pltpu.VMEM((REPL, NB, ROWS, HALF), jnp.bfloat16)] * CHUNKS,
         compiler_params=pltpu.CompilerParams(
             collective_id=0, has_side_effects=True, vmem_limit_bytes=VMEM_BYTES),

time: 85.8 us -> 81.7 us (0.952); the launches traced: 85.6 us -> 80.5 us
  Pallas kernels: 83 us -> 77.8 us
    pallas_call x1, Pallas kernels: 79.3 us -> 73.9 us  [local(): pl.pallas_call(functools.partial(exchange_kernel, sections, tensors), out...]
where the time goes in v3:
time: 81.7 us; the launch traced here: 80.5 us
  Pallas kernels  77.8 us (95%)
  local copies, waits for them, and re-layouts  2.6 us (3%)
    pallas_call x1, Pallas kernels, local(): pl.pallas_call(functools.partial(exchange_kernel, sections, tensors), out...  73.9 us
    pallas_call x1, Pallas kernels, attention(): pl.pallas_call(attention_kernel, out_shape=jax.ShapeDtypeStruct((rows, GQ...  3.92 us
    unnamed x6, local copies, waits for them, and re-layouts  2.6 us

profile of v3, /device:TPU:8, one launch (start us, length us, event | category | flops | bytes accessed | tf_op | source)
XLA Modules:
  0.0 80.5 jit_solution(12375206837978637334)
XLA Ops:
  0.0 0.0 copy-start
  0.0 1.2 %copy-done = bf16[1,4,1,128,1024]{4,3,2,1,0:T(8,128)(2,1)S(1)} copy-done((bf16[1,4,1,128,1024]{4,3,2,1,0:T(8,128)(2,1)S(1)}, bf16[1,4,1,128,1024]{4,3,2,1,0:T(8,128)(2,1)}, u32[]{:S(2)}) %copy-start) | copy-done | bytes 1048600
  1.2 0.0 copy-start.1
  1.2 0.7 copy-done.1
  1.9 0.0 copy-start.2
  1.9 0.7 copy-done.2
  2.6 73.9 %shard_map.46.qkv_ref = bf16[512,1280]{1,0:T(8,128)(2,1)S(1)} custom-call(bf16[4,128,1024]{2,1,0:T(8,128)(2,1)S(1)} %bitcast.4, bf16[4096,1280]{1,0:T(8,128)(2,1)} %bitcast.7, s32[4,4,16]{2,1,0:T(4,128)S(1)} %bitcast.5, s32[4,64]{1,0:T(4,128)S(1)} %copy-done.2), custom_call_target="tpu_custom_call" | custom-call | flops 5368709120 | bytes 13107200 | tf_op jit(solution)/shard_map/pallas_call | solution.py:387
  76.5 3.9 %shard_map.47 = bf16[512,1024]{1,0:T(8,128)(2,1)} custom-call(bf16[512,1280]{1,0:T(8,128)(2,1)S(1)} %shard_map.46.qkv_ref, s32[4,4,16]{2,1,0:T(4,128)S(1)} %bitcast.6, s32[4,64]{1,0:T(4,128)S(1)} %copy-done.2), custom_call_target="tpu_custom_call" | custom-call | flops 1073741824 | bytes 2621440 | tf_op jit(solution)/shard_map/pallas_call | solution.py:365
Async XLA Ops:
  0.0 1.2 %copy-start = (bf16[1,4,1,128,1024]{4,3,2,1,0:T(8,128)(2,1)S(1)}, bf16[1,4,1,128,1024]{4,3,2,1,0:T(8,128)(2,1)}, u32[]{:S(2)}) copy-start(bf16[1,4,1,128,1024]{4,3,2,1,0:T(8,128)(2,1)} %param.4) | copy-start | bytes 3145732
  1.2 0.7 copy-start.1
  1.9 0.7 copy-start.2

commit v4 on v3

--- a/solution.py
+++ b/solution.py
@@ -28,7 +28,7 @@
 EARLY = 1
 SPLIT = 1
 SLOTS = NB // SPLIT
-VMEM_BYTES = 48 * 1024 * 1024
+VMEM_BYTES = 60 * 1024 * 1024
 GROUP = 8
 
 norm_eps = 1e-05
@@ -37,9 +37,16 @@
 
 
 def far_first(step, chip, core):
-    size = (step + 1) // 2
-    offset = (1 - step % 2) * (CHIPS // 2 - size) - (step % 2) * (size % (CHIPS // 2))
-    return (chip + CHIPS + (1 - 2 * core) * offset) % CHIPS
+    size = lax.div(step + 1, 2)
+    odd = lax.rem(step, 2)
+    offset = (1 - odd) * (CHIPS // 2 - size) - odd * lax.rem(size, CHIPS // 2)
+    return lax.rem(chip + CHIPS + (1 - 2 * core) * offset, CHIPS)
+
+
+def near_first(step, chip, core):
+    size = lax.div(step + 1, 2)
+    offset = (2 * lax.rem(step, 2) - 1) * size
+    return lax.rem(chip + CHIPS + (1 - 2 * core) * offset, CHIPS)
 
 
 def slot_docs(bs_ref, len_ref, section, block, offset_iota):
@@ -122,8 +129,8 @@
 
     def spread(c):
         def send(e, carry):
-            to_chip = far_first(e % CHIPS, chip, core)
-            to_core = (e // CHIPS + 1 + core) % 2
+            to_chip = far_first(lax.rem(e, CHIPS), chip, core)
+            to_core = lax.rem(lax.div(e, CHIPS) + 1 + core, 2)
             pltpu.make_async_remote_copy(
                 src_ref=sbuf.at[c, to_core, to_chip],
                 dst_ref=mid[c].at[i],
@@ -138,7 +145,7 @@
 
     def pick(c, j, k):
         block = bs_ref[s, j * NB + k]
-        return mid[c][block % REPL, block // REPL]
+        return mid[c][lax.rem(block, REPL), lax.div(block, REPL)]
 
     def deliver(c):
         pltpu.make_async_copy(mid[c], mid[c], p1_recv.at[c]).wait()
@@ -146,12 +153,15 @@
         for part in range(SPLIT):
             slots = range(part * SLOTS, (part + 1) * SLOTS)
 
-            def send(e, carry):
-                to_chip = far_first((e - 1) % CHIPS, chip, core)
-                to_core = ((e - 1) // CHIPS + 1 + core) % 2
-                j = to_chip * 2 + to_core
+            def choose(j, carry):
                 for k in slots:
                     obuf[c, part, j, k % SLOTS] = pick(c, j, k)
+                return carry
+
+            def send(e, carry):
+                to_chip = near_first(lax.div(e, 2), chip, core)
+                to_core = lax.rem(e + core, 2)
+                j = to_chip * 2 + to_core
                 pltpu.make_async_remote_copy(
                     src_ref=obuf.at[c, part, j],
                     dst_ref=x.at[t, c, part, core, chip],
@@ -162,6 +172,7 @@
                 ).start()
                 return carry
 
+            lax.fori_loop(0, REPL, choose, 0)
             lax.fori_loop(1, REPL, send, 0)
             for k in slots:
                 x[t, c, part, core, chip, k % SLOTS] = pick(c, i, k)
@@ -306,7 +317,9 @@
                 y_copy(way, c, part).wait_send()
 
 
-def attention_kernel(qkv_ref, len_ref, bs_ref, out_ref, keys, values, context, out_sem):
+def attention_kernel(qkv_in, len_ref, bs_ref, out_ref, qkv_ref, keys, values, context, in_sem, out_sem):
+    fetch = pltpu.make_async_copy(qkv_in, qkv_ref, in_sem)
+    fetch.start()
     s = lax.axis_index("section")
     i = lax.axis_index("dp")
     blocks = [bs_ref[s, i * NB + k] for k in range(NB)]
@@ -317,6 +330,7 @@
     down = lax.broadcasted_iota(jnp.int32, (BLK, 1), 0)
     key_docs = [slot_docs(bs_ref, len_ref, s, block, across) for block in ordered]
     slot_rows = [pl.ds(pl.multiple_of(slot * BLK, BLK), BLK) for slot in slots]
+    fetch.wait()
     for r in range(NB):
         keys[:, r * BLK:(r + 1) * BLK] = qkv_ref[slot_rows[r], GQ * HD:(GQ + 1) * HD].T
         values[r * BLK:(r + 1) * BLK] = qkv_ref[slot_rows[r], (GQ + 1) * HD:]
@@ -365,15 +379,17 @@
     return pl.pallas_call(
         attention_kernel,
         out_shape=jax.ShapeDtypeStruct((rows, GQ * HD), jnp.bfloat16),
-        in_specs=[vmem, smem, smem],
+        in_specs=[pl.BlockSpec(memory_space=pltpu.HBM), smem, smem],
         out_specs=pl.BlockSpec(memory_space=pl.ANY),
         scratch_shapes=[
+            pltpu.VMEM((rows, COLS), jnp.bfloat16),
             pltpu.VMEM((HD, rows), jnp.bfloat16),
             pltpu.VMEM((rows, HD), jnp.bfloat16),
             pltpu.VMEM((NB, BLK, GQ * HD), jnp.bfloat16),
+            pltpu.SemaphoreType.DMA,
             pltpu.SemaphoreType.DMA((NB,)),
         ],
-        compiler_params=pltpu.CompilerParams(vmem_limit_bytes=32 * 1024 * 1024),
+        compiler_params=pltpu.CompilerParams(vmem_limit_bytes=VMEM_BYTES),
         cost_estimate=pl.CostEstimate(
             flops=4 * GQ * rows * rows * HD, bytes_accessed=rows * COLS * 4, transcendentals=GQ * rows * rows),
     )(qkv, by_document, block_source)

time: 81.7 us -> 81.1 us (level); the launches traced: 80.5 us -> 80.9 us
  Pallas kernels: 77.8 us -> 80.9 us
  local copies, waits for them, and re-layouts: 2.6 us -> 0 us
    unnamed x6 -> x0, local copies, waits for them, and re-layouts: 2.6 us -> none
    pallas_call x1, Pallas kernels: 3.92 us -> 5.84 us  [attention(): pl.pallas_call(attention_kernel, out_shape=jax.ShapeDtypeStruct((rows, GQ...]
    pallas_call x1, Pallas kernels: 73.9 us -> 75 us  [local(): pl.pallas_call(functools.partial(exchange_kernel, sections, tensors), out...]
where the time goes in v4:
time: 81.1 us; the launch traced here: 80.9 us
  Pallas kernels  80.9 us (100%)
    pallas_call x1, Pallas kernels, local(): pl.pallas_call(functools.partial(exchange_kernel, sections, tensors), out...  75 us
    pallas_call x1, Pallas kernels, attention(): pl.pallas_call(attention_kernel, out_shape=jax.ShapeDtypeStruct((rows, GQ...  5.84 us

profile of v4, /device:TPU:8, one launch (start us, length us, event | category | flops | bytes accessed | tf_op | source)
XLA Modules:
  0.0 80.9 jit_solution(6761448653110637252)
XLA Ops:
  0.0 75.0 %shard_map.46.qkv_in = bf16[512,1280]{1,0:T(8,128)(2,1)} custom-call(bf16[4,128,1024]{2,1,0:T(8,128)(2,1)} %bitcast.5, bf16[4096,1280]{1,0:T(8,128)(2,1)} %bitcast.4, s32[4,4,16]{2,1,0:T(4,128)} %bitcast.6, s32[4,64]{1,0:T(4,128)} %bs_ref.3), custom_call_target="tpu_custom_call" | custom-call | flops 5368709120 | bytes 13107200 | tf_op jit(solution)/shard_map/pallas_call | solution.py:403
  75.1 5.8 %shard_map.47 = bf16[512,1024]{1,0:T(8,128)(2,1)} custom-call(bf16[512,1280]{1,0:T(8,128)(2,1)} %shard_map.46.qkv_in, s32[4,4,16]{2,1,0:T(4,128)} %bitcast.7, s32[4,64]{1,0:T(4,128)} %bs_ref.3), custom_call_target="tpu_custom_call" | custom-call | flops 1073741824 | bytes 2621440 | tf_op jit(solution)/shard_map/pallas_call | solution.py:379

commit v5 on v4

--- a/solution.py
+++ b/solution.py
@@ -28,7 +28,7 @@
 EARLY = 1
 SPLIT = 1
 SLOTS = NB // SPLIT
-VMEM_BYTES = 60 * 1024 * 1024
+VMEM_BYTES = 48 * 1024 * 1024
 GROUP = 8
 
 norm_eps = 1e-05
@@ -66,8 +66,8 @@
 
 def exchange_kernel(
     sections, tensors, acts_ref, w_ref, len_ref, bs_ref, qkv_ref,
-    rows_in, sbuf, obuf, x, wv, acc, squares, cos_t, sin_t,
-    a_sem, w_sem, p1_send, p1_recv, p2_send, p2_recv, y_send, y_recv, *mid
+    sbuf, obuf, x, wv, acc, squares, cos_t, sin_t,
+    w_sem, p1_send, p1_recv, p2_send, p2_recv, y_send, y_recv, *mid
 ):
     s = lax.axis_index("section")
     i = lax.axis_index("dp")
@@ -79,12 +79,6 @@
     t_left = (t + tensors - 1) % tensors
     t_far = (t + 2) % tensors
 
-    def fetch(c):
-        return pltpu.make_async_copy(
-            acts_ref.at[:, :, pl.ds(c * FEAT, FEAT)], rows_in.at[c], a_sem.at[c])
-
-    for c in range(CHUNKS):
-        fetch(c).start()
     w_copy = pltpu.make_async_copy(w_ref, wv, w_sem)
     w_copy.start()
 
@@ -114,10 +108,9 @@
     signs = jnp.where((row_id // HB) == (col_id // HB), sign, 0.0).astype(jnp.bfloat16)
 
     def rotate(c):
-        fetch(c).wait()
         for part in range(FEAT // (2 * HB)):
-            first = part * 2 * HB
-            block_rows = rows_in[c, :, :, first:first + 2 * HB].reshape(NB * BLK, 2 * HB)
+            first = c * FEAT + part * 2 * HB
+            block_rows = acts_ref[:, :, first:first + 2 * HB].reshape(NB * BLK, 2 * HB)
             turned = jnp.dot(block_rows, signs, preferred_element_type=jnp.float32)
             low = (turned * (1.0 / math.sqrt(HB))).astype(jnp.bfloat16)
             for piece in range(2):
@@ -317,9 +310,7 @@
                 y_copy(way, c, part).wait_send()
 
 
-def attention_kernel(qkv_in, len_ref, bs_ref, out_ref, qkv_ref, keys, values, context, in_sem, out_sem):
-    fetch = pltpu.make_async_copy(qkv_in, qkv_ref, in_sem)
-    fetch.start()
+def attention_kernel(qkv_ref, len_ref, bs_ref, out_ref, keys, values, context, out_sem):
     s = lax.axis_index("section")
     i = lax.axis_index("dp")
     blocks = [bs_ref[s, i * NB + k] for k in range(NB)]
@@ -330,7 +321,6 @@
     down = lax.broadcasted_iota(jnp.int32, (BLK, 1), 0)
     key_docs = [slot_docs(bs_ref, len_ref, s, block, across) for block in ordered]
     slot_rows = [pl.ds(pl.multiple_of(slot * BLK, BLK), BLK) for slot in slots]
-    fetch.wait()
     for r in range(NB):
         keys[:, r * BLK:(r + 1) * BLK] = qkv_ref[slot_rows[r], GQ * HD:(GQ + 1) * HD].T
         values[r * BLK:(r + 1) * BLK] = qkv_ref[slot_rows[r], (GQ + 1) * HD:]
@@ -379,17 +369,15 @@
     return pl.pallas_call(
         attention_kernel,
         out_shape=jax.ShapeDtypeStruct((rows, GQ * HD), jnp.bfloat16),
-        in_specs=[pl.BlockSpec(memory_space=pltpu.HBM), smem, smem],
+        in_specs=[vmem, smem, smem],
         out_specs=pl.BlockSpec(memory_space=pl.ANY),
         scratch_shapes=[
-            pltpu.VMEM((rows, COLS), jnp.bfloat16),
             pltpu.VMEM((HD, rows), jnp.bfloat16),
             pltpu.VMEM((rows, HD), jnp.bfloat16),
             pltpu.VMEM((NB, BLK, GQ * HD), jnp.bfloat16),
-            pltpu.SemaphoreType.DMA,
             pltpu.SemaphoreType.DMA((NB,)),
         ],
-        compiler_params=pltpu.CompilerParams(vmem_limit_bytes=VMEM_BYTES),
+        compiler_params=pltpu.CompilerParams(vmem_limit_bytes=32 * 1024 * 1024),
         cost_estimate=pl.CostEstimate(
             flops=4 * GQ * rows * rows * HD, bytes_accessed=rows * COLS * 4, transcendentals=GQ * rows * rows),
     )(qkv, by_document, block_source)
@@ -403,10 +391,9 @@
     qkv = pl.pallas_call(
         functools.partial(exchange_kernel, sections, tensors),
         out_shape=jax.ShapeDtypeStruct((rows, COLS), jnp.bfloat16),
-        in_specs=[pl.BlockSpec(memory_space=pltpu.HBM)] * 2 + [smem] * 2,
+        in_specs=[vmem, pl.BlockSpec(memory_space=pltpu.HBM), smem, smem],
         out_specs=vmem,
         scratch_shapes=[
-            pltpu.VMEM((CHUNKS, NB, BLK, FEAT), jnp.bfloat16),
             pltpu.VMEM((CHUNKS, 2, CHIPS, NB, ROWS, HALF), jnp.bfloat16),
             pltpu.VMEM((CHUNKS, SPLIT, REPL, SLOTS, ROWS, HALF), jnp.bfloat16),
             pltpu.VMEM((4, CHUNKS, SPLIT, 2, CHIPS, SLOTS, ROWS, HALF), jnp.bfloat16),
@@ -415,7 +402,6 @@
             pltpu.VMEM((rows, HB), jnp.float32),
             pltpu.VMEM((SPLIT, CHIPS, SLOTS, ROWS, HD), jnp.float32),
             pltpu.VMEM((SPLIT, CHIPS, SLOTS, ROWS, HD), jnp.float32),
-            pltpu.SemaphoreType.DMA((CHUNKS,)),
             pltpu.SemaphoreType.DMA,
             pltpu.SemaphoreType.DMA((CHUNKS,)),
             pltpu.SemaphoreType.DMA((CHUNKS,)),

time: 81.1 us -> 80.8 us (level)
  Pallas kernels: 80.9 us -> 77.8 us
  local copies, waits for them, and re-layouts: 0 us -> 2.6 us
    unnamed x0 -> x6, local copies, waits for them, and re-layouts: none -> 2.6 us
    pallas_call x1, Pallas kernels: 5.84 us -> 3.91 us  [attention(): pl.pallas_call(attention_kernel, out_shape=jax.ShapeDtypeStruct((rows, GQ...]
    pallas_call x1, Pallas kernels: 75 us -> 73.9 us  [local(): pl.pallas_call(functools.partial(exchange_kernel, sections, tensors), out...]
where the time goes in v5:
time: 80.8 us; the launch traced here: 80.4 us
  Pallas kernels  77.8 us (96%)
  local copies, waits for them, and re-layouts  2.6 us (3%)
    pallas_call x1, Pallas kernels, local(): pl.pallas_call(functools.partial(exchange_kernel, sections, tensors), out...  73.9 us
    pallas_call x1, Pallas kernels, attention(): pl.pallas_call(attention_kernel, out_shape=jax.ShapeDtypeStruct((rows, GQ...  3.91 us
    unnamed x6, local copies, waits for them, and re-layouts  2.6 us

profile of v5, /device:TPU:8, one launch (start us, length us, event | category | flops | bytes accessed | tf_op | source)
XLA Modules:
  0.0 80.4 jit_solution(8454006124758610613)
XLA Ops:
  0.0 0.0 copy-start
  0.0 1.2 %copy-done = bf16[1,4,1,128,1024]{4,3,2,1,0:T(8,128)(2,1)S(1)} copy-done((bf16[1,4,1,128,1024]{4,3,2,1,0:T(8,128)(2,1)S(1)}, bf16[1,4,1,128,1024]{4,3,2,1,0:T(8,128)(2,1)}, u32[]{:S(2)}) %copy-start) | copy-done | bytes 1048600
  1.2 0.0 copy-start.1
  1.2 0.7 copy-done.1
  1.9 0.0 copy-start.2
  1.9 0.7 copy-done.2
  2.6 73.9 %shard_map.46.qkv_ref = bf16[512,1280]{1,0:T(8,128)(2,1)S(1)} custom-call(bf16[4,128,1024]{2,1,0:T(8,128)(2,1)S(1)} %bitcast.4, bf16[4096,1280]{1,0:T(8,128)(2,1)} %bitcast.7, s32[4,4,16]{2,1,0:T(4,128)S(1)} %bitcast.5, s32[4,64]{1,0:T(4,128)S(1)} %copy-done.2), custom_call_target="tpu_custom_call" | custom-call | flops 5368709120 | bytes 13107200 | tf_op jit(solution)/shard_map/pallas_call | solution.py:391
  76.5 3.9 %shard_map.47 = bf16[512,1024]{1,0:T(8,128)(2,1)} custom-call(bf16[512,1280]{1,0:T(8,128)(2,1)S(1)} %shard_map.46.qkv_ref, s32[4,4,16]{2,1,0:T(4,128)S(1)} %bitcast.6, s32[4,64]{1,0:T(4,128)S(1)} %copy-done.2), custom_call_target="tpu_custom_call" | custom-call | flops 1073741824 | bytes 2621440 | tf_op jit(solution)/shard_map/pallas_call | solution.py:369
Async XLA Ops:
  0.0 1.2 %copy-start = (bf16[1,4,1,128,1024]{4,3,2,1,0:T(8,128)(2,1)S(1)}, bf16[1,4,1,128,1024]{4,3,2,1,0:T(8,128)(2,1)}, u32[]{:S(2)}) copy-start(bf16[1,4,1,128,1024]{4,3,2,1,0:T(8,128)(2,1)} %param.4) | copy-start | bytes 3145732
  1.2 0.7 copy-start.1
  1.9 0.7 copy-start.2

commit v6 on v4

--- a/solution.py
+++ b/solution.py
@@ -28,7 +28,7 @@
 EARLY = 1
 SPLIT = 1
 SLOTS = NB // SPLIT
-VMEM_BYTES = 60 * 1024 * 1024
+VMEM_BYTES = 48 * 1024 * 1024
 GROUP = 8
 
 norm_eps = 1e-05
@@ -317,9 +317,7 @@
                 y_copy(way, c, part).wait_send()
 
 
-def attention_kernel(qkv_in, len_ref, bs_ref, out_ref, qkv_ref, keys, values, context, in_sem, out_sem):
-    fetch = pltpu.make_async_copy(qkv_in, qkv_ref, in_sem)
-    fetch.start()
+def attention_kernel(qkv_ref, len_ref, bs_ref, out_ref, keys, values, context, out_sem):
     s = lax.axis_index("section")
     i = lax.axis_index("dp")
     blocks = [bs_ref[s, i * NB + k] for k in range(NB)]
@@ -330,7 +328,6 @@
     down = lax.broadcasted_iota(jnp.int32, (BLK, 1), 0)
     key_docs = [slot_docs(bs_ref, len_ref, s, block, across) for block in ordered]
     slot_rows = [pl.ds(pl.multiple_of(slot * BLK, BLK), BLK) for slot in slots]
-    fetch.wait()
     for r in range(NB):
         keys[:, r * BLK:(r + 1) * BLK] = qkv_ref[slot_rows[r], GQ * HD:(GQ + 1) * HD].T
         values[r * BLK:(r + 1) * BLK] = qkv_ref[slot_rows[r], (GQ + 1) * HD:]
@@ -379,17 +376,15 @@
     return pl.pallas_call(
         attention_kernel,
         out_shape=jax.ShapeDtypeStruct((rows, GQ * HD), jnp.bfloat16),
-        in_specs=[pl.BlockSpec(memory_space=pltpu.HBM), smem, smem],
+        in_specs=[vmem, smem, smem],
         out_specs=pl.BlockSpec(memory_space=pl.ANY),
         scratch_shapes=[
-            pltpu.VMEM((rows, COLS), jnp.bfloat16),
             pltpu.VMEM((HD, rows), jnp.bfloat16),
             pltpu.VMEM((rows, HD), jnp.bfloat16),
             pltpu.VMEM((NB, BLK, GQ * HD), jnp.bfloat16),
-            pltpu.SemaphoreType.DMA,
             pltpu.SemaphoreType.DMA((NB,)),
         ],
-        compiler_params=pltpu.CompilerParams(vmem_limit_bytes=VMEM_BYTES),
+        compiler_params=pltpu.CompilerParams(vmem_limit_bytes=32 * 1024 * 1024),
         cost_estimate=pl.CostEstimate(
             flops=4 * GQ * rows * rows * HD, bytes_accessed=rows * COLS * 4, transcendentals=GQ * rows * rows),
     )(qkv, by_document, block_source)

time: 81.1 us -> 81 us (level)
  local copies, waits for them, and re-layouts: 0 us -> 2.6 us
  Pallas kernels: 80.9 us -> 78.4 us
    unnamed x0 -> x6, local copies, waits for them, and re-layouts: none -> 2.6 us
    pallas_call x1, Pallas kernels: 5.84 us -> 4.41 us  [attention(): pl.pallas_call(attention_kernel, out_shape=jax.ShapeDtypeStruct((rows, GQ...]
    pallas_call x1, Pallas kernels: 75 us -> 74 us  [local(): pl.pallas_call(functools.partial(exchange_kernel, sections, tensors), out...]
where the time goes in v6:
time: 81 us
  Pallas kernels  78.4 us (97%)
  local copies, waits for them, and re-layouts  2.6 us (3%)
    pallas_call x1, Pallas kernels, local(): pl.pallas_call(functools.partial(exchange_kernel, sections, tensors), out...  74 us
    pallas_call x1, Pallas kernels, attention(): pl.pallas_call(attention_kernel, out_shape=jax.ShapeDtypeStruct((rows, GQ...  4.41 us
    unnamed x6, local copies, waits for them, and re-layouts  2.6 us

profile of v6, /device:TPU:8, one launch (start us, length us, event | category | flops | bytes accessed | tf_op | source)
XLA Modules:
  0.0 81.0 jit_solution(11055112125525533722)
XLA Ops:
  0.0 0.0 copy-start
  0.0 1.2 %copy-done = bf16[1,4,1,128,1024]{4,3,2,1,0:T(8,128)(2,1)S(1)} copy-done((bf16[1,4,1,128,1024]{4,3,2,1,0:T(8,128)(2,1)S(1)}, bf16[1,4,1,128,1024]{4,3,2,1,0:T(8,128)(2,1)}, u32[]{:S(2)}) %copy-start) | copy-done | bytes 1048600
  1.2 0.0 copy-start.1
  1.2 0.7 copy-done.1
  1.9 0.0 copy-start.2
  1.9 0.7 copy-done.2
  2.6 74.0 %shard_map.46.qkv_ref = bf16[512,1280]{1,0:T(8,128)(2,1)S(1)} custom-call(bf16[4,128,1024]{2,1,0:T(8,128)(2,1)S(1)} %bitcast.4, bf16[4096,1280]{1,0:T(8,128)(2,1)} %bitcast.7, s32[4,4,16]{2,1,0:T(4,128)S(1)} %bitcast.5, s32[4,64]{1,0:T(4,128)S(1)} %copy-done.2), custom_call_target="tpu_custom_call" | custom-call | flops 5368709120 | bytes 13107200 | tf_op jit(solution)/shard_map/pallas_call | solution.py:398
  76.6 4.4 %shard_map.47 = bf16[512,1024]{1,0:T(8,128)(2,1)} custom-call(bf16[512,1280]{1,0:T(8,128)(2,1)S(1)} %shard_map.46.qkv_ref, s32[4,4,16]{2,1,0:T(4,128)S(1)} %bitcast.6, s32[4,64]{1,0:T(4,128)S(1)} %copy-done.2), custom_call_target="tpu_custom_call" | custom-call | flops 1073741824 | bytes 2621440 | tf_op jit(solution)/shard_map/pallas_call | solution.py:376
Async XLA Ops:
  0.0 1.2 %copy-start = (bf16[1,4,1,128,1024]{4,3,2,1,0:T(8,128)(2,1)S(1)}, bf16[1,4,1,128,1024]{4,3,2,1,0:T(8,128)(2,1)}, u32[]{:S(2)}) copy-start(bf16[1,4,1,128,1024]{4,3,2,1,0:T(8,128)(2,1)} %param.4) | copy-start | bytes 3145732
  1.2 0.7 copy-start.1
  1.9 0.7 copy-start.2
